TPU v7x, 32 devices: a whole 2x2x4 slice. The times are simulated.
32 devices in a mesh: seq: 8 (over z, y), grp: 4 (over x, core).
Axes of the slice: x: 2, y: 2, z: 4, core: 2. Of those that a mesh axis runs over, the one named last changes fastest.
Arguments:
- frames_in: bfloat16 [4, 5120, 512], P('grp', 'seq'), may hold values from -6 to 6
- cond_frames: bfloat16 [4, 5120, 512], P('grp', 'seq'), may hold values from -6 to 6
- step_embed: bfloat16 [4, 512], P('grp'), may hold values from -6 to 6
- prompts: bfloat16 [16, 512, 512], replicated, may hold values from -6 to 6
- prompt_lengths: int32 [16], replicated, may hold values from 1 to 512, 5120 in all
- pairing: int32 [4], P('grp'), may hold values from 0 to 15
- dilations: int32 [2], replicated, may hold values from 1 to 8, as said below
- owners: int32 [34], replicated, may hold values from 0 to 3, as said below
- master: float32 [52, 512, 512], P('grp', 'seq')
- first_moment: float32 [52, 512, 512], P('grp', 'seq'), may hold values from -20 to 20
- second_moment: float32 [52, 512, 512], P('grp', 'seq'), may hold values from 0.8192 to 3.2768
- queries: float32 [2, 32, 512], replicated, may hold values from -6 to 6
- query_first: float32 [2, 32, 512], replicated, may hold values from -4 to 4
- query_second: float32 [2, 32, 512], replicated, may hold values from 0.008192 to 0.032768
- grad_out: bfloat16 [4, 5120, 512], P('grp', 'seq'), may hold values from -6 to 6
- grad_skip: bfloat16 [4, 5120, 512], P('grp', 'seq'), may hold values from -6 to 6
Outputs:
- new_first: float32 [52, 512, 512], P('grp', 'seq')
- new_second: float32 [52, 512, 512], P('grp', 'seq')
- new_master: float32 [52, 512, 512], P('grp', 'seq')
- new_copy: bfloat16 [52, 512, 512], P('grp', 'seq')
- new_query_first: float32 [2, 32, 512], replicated
- new_query_second: float32 [2, 32, 512], replicated
- new_queries: float32 [2, 32, 512], replicated
- block_out: float32 [4, 5120, 512], P('grp', 'seq')
- skip_out: float32 [4, 5120, 512], P('grp', 'seq')
- grad_frames: float32 [4, 5120, 512], P('grp', 'seq')
Inputs may be any that keep to these rules, and one draw needn't show every extreme that they name: The owners hold 13, 9, 7 and 5 matrices, in an order that varies. `dilations`: one layer has dilation 8.
All inputs are finite; a program needn't handle non-finite values.
Results may differ from a plain program's by a relative error of at most 0.017.
Values may be sent and summed in bfloat16 or wider, within the bound.
A program may use at most 192 MiB of HBM per device.

v0:
```python
import functools

import jax
import jax.numpy as jnp
from jax import lax
from jax.experimental import pallas as pl
from jax.experimental.pallas import tpu as pltpu
from jax.sharding import PartitionSpec as P

HEADS = 8
LAYERS = 2
DMAX = 8
CAP = 13
STEP = 10
PER_LAYER = 17
TILES = PER_LAYER * LAYERS

BETA_ONE = 0.9
BETA_TWO = 0.999
EPSILON = 1e-08
WEIGHT_DECAY = 0.01
LEARN_RATE = 0.02
QUERY_RATE = 0.4
HALF_ROOT = 0.7071067811865476
NEGATIVE = -1e30

BF = jnp.bfloat16
F32 = jnp.float32
HALO = 32
WIDE = 256
MAIN = 20
BLOCKS = MAIN * LAYERS
PHASES = (None, (0, MAIN), (MAIN, MAIN))
FILM_ORDER = (10, 11, 12, 13, 14, 8, 9)
FILM = 2 * len(FILM_ORDER)
LOW_RANK = len(FILM_ORDER)
KEY_VALUE = 4 * LAYERS
HOP_ROWS = (24, 16, 32, 8, 8)
IN_SPLIT = (2, 2, 2)
OUT_SPLIT = (2, 2)
LAST_DIRECT = True
ORDER = (
    ("prep", 1), "fcK", "fcR", ("pr", 0), ("prep", 2), ("cross", 1), "fxK", ("pr", 1),
    ("cross", 2), "fxR", ("end", 1), ("first", 1, 0), "flK", ("pr", 2), "hsK", ("end", 2),
    ("first", 2, 0), ("first", 1, 2), ("first", 1, 1), ("pr", 3), ("first", 1, 3), "flR",
    ("second", 1, 2), ("second", 1, 0), "heK", ("second", 2, 0), "att", ("second", 1, 1), "hsB",
    ("second", 1, 3), ("first", 2, 2), ("first", 2, 3), ("third", 1, 3), ("third", 2, 0), "heB",
    ("third", 1, 2), "hsC", ("third", 1, 1), ("third", 1, 0), ("first", 2, 1), ("second", 2, 2),
    "heC", ("second", 2, 3), "win0", "condt", ("second", 2, 1), "gates0a", "gates0b",
    ("third", 2, 2), "res0", ("third", 2, 3), ("third", 2, 1), "gatt0", "skip0", "win1",
    "gates1a", "gates1b", "gatt1", "gg1a", "gg1b", "winb1", ("give", 1, 1), ("give", 1, 0),
    "fg1a", ("keep", 1, 1), "fg1b", ("keep", 1, 0), ("one", 1, 3), "gg0a", ("one", 1, 1), "gg0b",
    "winb0", "out1", "fg0b", ("one", 1, 0), ("one", 1, 2), ("give", 0, 0), "fg0a", "hs3",
    ("two", 1, 3), ("give", 0, 1), ("two", 1, 1), ("keep", 0, 0), ("two", 1, 2), ("two", 1, 0),
    ("keep", 0, 1), "he3", ("one", 0, 2), ("one", 0, 0), "hs4", ("three", 1, 1), ("one", 0, 1),
    ("three", 1, 2), ("one", 0, 3), ("three", 1, 3), ("two", 0, 2), "he4", "fb", "dq1", "hs5",
    ("two", 0, 0), ("three", 1, 0), ("two", 0, 1), ("two", 0, 3), ("three", 0, 2),
    ("three", 0, 0), ("three", 0, 1), ("three", 0, 3), "he5", "bundle", ("four", 1), "dq2",
    ("four", 0), ("five", 1), "dq3", "low", "end",
)

MEM = 64 * 1024 * 1024 - 256 * 1024
MESH = pl.DeviceIdType.MESH


def block_table():
    table = {}
    for layer in range(LAYERS):
        base = PER_LAYER * layer
        start = MAIN * layer
        for part in range(4):
            for tap in range(4):
                table[base + 2 * tap + part // 2, part % 2] = start + 5 * part + tap
            table[base + 15 + part // 2, part % 2] = start + 5 * part + 4
    return table


BLOCK_OF = block_table()
FILM_OF = {
    (PER_LAYER * layer + tile, side): (
        4 * layer + 2 * place + side
        if place < 2
        else KEY_VALUE + (FILM - 4) * layer + 2 * (place - 2) + side
    )
    for layer in range(LAYERS)
    for place, tile in enumerate(FILM_ORDER)
    for side in range(2)
}


def mm(a, b):
    return lax.dot_general(a, b, (((1,), (0,)), ((), ())), preferred_element_type=F32)


def mm_nt(a, b):
    return lax.dot_general(a, b, (((1,), (1,)), ((), ())), preferred_element_type=F32)


def mm_nt_fine(a, b):
    high = a.astype(BF)
    return mm_nt(high, b) + mm_nt((a - high.astype(F32)).astype(BF), b)


def mm_low(a, b):
    return mm(a.astype(BF), b)


def mm_nt_low(a, b):
    return mm_nt(a.astype(BF), b)


def mm_nt_pairs(a, blocks):
    total = None
    for place, block in enumerate(blocks):
        term = mm_nt_fine(a[:, place * WIDE : (place + 1) * WIDE], block)
        total = term if total is None else total + term
    return total


def window(ref, start, count, width):
    group, rest = lax.div(start, 8), lax.rem(start, 8)
    groups = ref[pl.ds(group, count // 8 + 1), :, 0:width]
    turned = pltpu.roll(groups, lax.rem(8 - rest, 8), 1)
    row = lax.broadcasted_iota(jnp.int32, (1, 8, 1), 1)
    return jnp.where(row < 8 - rest, turned[:-1], turned[1:]).reshape(count, width)


def in_eights(value):
    return value.reshape(value.shape[0] // 8, 8, value.shape[1])


def place_of(n_seq):
    seq, grp = lax.axis_index("seq"), lax.axis_index("grp")
    z, y = lax.div(seq, 2), lax.rem(seq, 2)
    x, c = lax.div(grp, 2), lax.rem(grp, 2)
    return seq, grp, z, y, x, c


def greet(n_seq, seq, grp, groups):
    barrier = pltpu.get_barrier_semaphore()

    def one(k, carry):
        pl.semaphore_signal(
            barrier, inc=1, device_id={"seq": lax.rem(seq + k, n_seq), "grp": grp}, device_id_type=MESH
        )
        return carry

    lax.fori_loop(1, n_seq, one, 0)
    for k in range(1, groups):
        pl.semaphore_signal(
            barrier, inc=1, device_id={"seq": seq, "grp": lax.rem(grp + k, groups)}, device_id_type=MESH
        )
    pl.semaphore_wait(barrier, n_seq - 1 + groups - 1)


def any_spec():
    return pl.BlockSpec(memory_space=pl.ANY)


def vmem_spec():
    return pl.BlockSpec(memory_space=pltpu.VMEM)


def smem_spec():
    return pl.BlockSpec(memory_space=pltpu.SMEM)


def head_mask():
    row = lax.broadcasted_iota(jnp.int32, (HEADS, 512), 0)
    column = lax.broadcasted_iota(jnp.int32, (HEADS, 512), 1)
    return lax.div(column, 512 // HEADS) == row


def block_diagonal(rows):
    column = lax.div(lax.broadcasted_iota(jnp.int32, rows.shape, 1), 512 // HEADS)
    return jnp.concatenate([jnp.where(column == h, rows, 0.0) for h in range(HEADS)], axis=0)


def same_rows(row):
    return jnp.broadcast_to(row, (8, row.shape[1]))


def pack(vectors):
    pieces = [v[:, 128 * i : 128 * (i + 1)] for v in vectors for i in range(v.shape[1] // 128)]
    spare = -len(pieces) % 8
    if spare:
        pieces.append(jnp.zeros((spare, 128), pieces[0].dtype))
    return jnp.concatenate(pieces, axis=0)


def unpack(rows, place, pieces=4):
    return jnp.concatenate(
        [rows[pieces * place + i : pieces * place + i + 1] for i in range(pieces)], axis=1
    )


def step_kernel(
    n_seq, owners_ref, dil_ref, lengths_ref, pairing_ref, embed_ref, queries_ref, master_hbm,
    prompts_hbm, frames_hbm, cond_hbm, gout_hbm, gskip_hbm,
    block_hbm, skip_hbm, gframes_hbm, out_hbm, low_ref, dquery_ref,
    w, gs, prep, core_in, x_in, fr, fr_in, fx, ff, red_in, one_in, two_in, z_in, fin,
    xe, cat, slopes, gated, x1, bh, bb, sht, condt, gatt, bx, sk,
    master, prompt, probs, left, vec, sums, bundle, wide, dq_in,
    kv_out, kv_in, at_out, at_in, small_out, small_in, dq_out, dq_all, hop_src, hop_in,
    in_sem, prompt_sem, out_sem, hsend, hrecv, send, recv, hop_send, hop_recv, each_send, each_recv,
):
    seq, grp, z, y, x, c = place_of(n_seq)
    nz = n_seq // 2
    rows = prep.shape[1]
    own = frames_hbm.shape[1]
    grid_rows = own + 2 * HALO
    top = HALO + own
    channels = 512
    number = queries_ref.shape[1]
    sib, across, other_y = x * 2 + 1 - c, (1 - x) * 2 + c, z * 2 + 1 - y
    mine, theirs = 2 * c + x, 2 * c + 1 - x

    local_in = [
        pltpu.make_async_copy(a, b, in_sem.at[i])
        for i, (a, b) in enumerate(
            (
                (master_hbm, master),
                (frames_hbm.at[0], xe.at[pl.ds(HALO, own)]),
                (cond_hbm.at[0], cat.at[pl.ds(HALO, own), pl.ds(1536, channels)]),
                (gout_hbm.at[0], bb.at[pl.ds(HALO, own), pl.ds(0, channels)]),
                (gskip_hbm.at[0], bb.at[pl.ds(HALO, own), pl.ds(channels, channels)]),
            )
        )
    ]
    for copy in local_in:
        copy.start()

    def prompt_copy(turn, i):
        rows_now, columns = pl.ds(0, prompt.shape[0]), pl.ds((i % 2) * channels, channels)
        return pltpu.make_async_copy(
            prompts_hbm.at[4 * turn + i], slopes.at[i // 2, rows_now, columns], prompt_sem.at[i]
        )

    for i in range(4):
        prompt_copy(0, i).start()

    greet(n_seq, seq, grp, 4)

    waits = []
    used = [0]

    def remote(src, dst, to_seq, to_grp, sent=None):
        place = used[0]
        used[0] += 1
        copy = pltpu.make_async_remote_copy(
            src_ref=src,
            dst_ref=dst,
            send_sem=send.at[place],
            recv_sem=recv.at[place],
            device_id={"seq": to_seq, "grp": to_grp},
            device_id_type=MESH,
        )
        copy.start()
        (waits if sent is None else sent).append(copy)
        return copy

    after, before = lax.rem(seq + 1, n_seq), lax.rem(seq + n_seq - 1, n_seq)
    halos = []
    for ref, buffer, column in (
        (frames_hbm, xe, 0),
        (cond_hbm, cat, 1536),
        (gout_hbm, bb, 0),
        (gskip_hbm, bb, channels),
    ):
        for start, at, target in ((own - HALO, 0, after), (0, top, before)):
            place = len(halos)
            copy = pltpu.make_async_remote_copy(
                src_ref=ref.at[0, pl.ds(start, HALO)],
                dst_ref=buffer.at[pl.ds(at, HALO), pl.ds(column, channels)],
                send_sem=hsend.at[place],
                recv_sem=hrecv.at[place],
                device_id={"seq": target, "grp": grp},
                device_id_type=MESH,
            )
            copy.start()
            halos.append(copy)

    slots, flags = [], []
    count = jnp.int32(0)
    for tile in range(TILES):
        flag = (owners_ref[tile] == grp).astype(jnp.int32)
        slots.append(jnp.minimum(count, CAP - 1))
        flags.append(flag.astype(F32))
        count = count + flag

    def rounded(tile):
        return (master[slots[tile]] * flags[tile]).astype(BF)

    def ready(tiles, buffer, table):
        for tile in tiles:
            value = rounded(tile)
            buffer[table[tile, 0]] = value[:, :WIDE]
            buffer[table[tile, 1]] = value[:, WIDE:]

    def merge_start(phase):
        base, blocks = PHASES[phase]
        each = blocks // 4
        return remote(
            prep.at[pl.ds(base + 2 * (1 - c) * each, 2 * each)],
            core_in.at[pl.ds(base // 2, 2 * each)],
            seq, sib,
        )

    def merge_cross(phase, copy):
        base, blocks = PHASES[phase]
        each = blocks // 4
        copy.wait_recv()

        def add(i, carry):
            place = base // 2 + i
            core_in[place] = core_in[place] + prep[base + 2 * c * each + i]
            return carry

        lax.fori_loop(0, 2 * each, add, 0)
        return remote(
            core_in.at[pl.ds(base // 2 + (1 - x) * each, each)],
            x_in.at[pl.ds(base // 4, each)],
            seq, across,
        )

    def view(phase, quarter, zz, yy):
        base, blocks = PHASES[phase]
        each = blocks // 4
        return w.at[pl.ds(base + quarter * each, each), zz, yy]

    gathering, legs = [], {}

    def spread(ref, to_seq, to_grp):
        return remote(ref, ref, to_seq, to_grp, gathering)

    def merge_end(phase, copy):
        base, blocks = PHASES[phase]
        each = blocks // 4
        copy.wait_recv()

        def settle(i, carry):
            w[base + mine * each + i, z, y] = (
                core_in[base // 2 + x * each + i] + x_in[base // 4 + i]
            )
            return carry

        lax.fori_loop(0, each, settle, 0)

    def y_first(zz, quarters):
        return 1 - jnp.minimum(lax.div(4 * zz, quarters * nz), 1)

    def spread_z(phase):
        ref = view(phase, mine, z, y)
        for k in range(1, nz):
            legs[phase, k] = spread(ref, lax.rem(z + k, nz) * 2 + y, grp)

    core_legs = {phase: [] for phase in (1, 2)}

    def first(phase, k):
        zs = lax.rem(z - k + nz, nz)
        a = y_first(zs, IN_SPLIT[phase])
        b = 1 - a
        if k:
            legs[phase, k].wait_recv()
        ref = view(phase, mine, zs, y)
        one = spread(ref, a * other_y + b * seq, a * grp + b * across)
        two = spread(ref, a * seq + b * other_y, a * across + b * grp)
        core_legs[phase].append(spread(ref, seq, sib))
        legs[phase, k] = (zs, a, one, two)

    def second(phase, k):
        zs, a, one, two = legs[phase, k]
        b = 1 - a
        one.wait_recv()
        ref = view(phase, a * mine + b * theirs, zs, a * (1 - y) + b * y)
        last = spread(ref, a * seq + b * other_y, a * across + b * grp)
        core_legs[phase].append(spread(ref, seq, sib))
        legs[phase, k] = (zs, a, two, last)

    def third(phase, k):
        zs, a, two, last = legs[phase, k]
        b = 1 - a
        two.wait_recv()
        ref = view(phase, a * theirs + b * mine, zs, a * y + b * (1 - y))
        core_legs[phase].append(spread(ref, seq, sib))
        last.wait_recv()
        core_legs[phase].append(spread(view(phase, theirs, zs, 1 - y), seq, sib))

    def arrived(phase):
        for copy in core_legs[phase]:
            copy.wait_recv()

    def hop_refs(j):
        start = sum(HOP_ROWS[:j])
        spot = pl.ds(start, HOP_ROWS[j])
        return hop_src.at[spot], hop_in.at[seq, spot], hop_in.at[:, spot]

    def hop_copy(j, k):
        src, dst, _ = hop_refs(j)
        return pltpu.make_async_remote_copy(
            src_ref=src,
            dst_ref=dst,
            send_sem=hop_send.at[j, k],
            recv_sem=hop_recv.at[j, k],
            device_id={"seq": lax.rem(seq + k, n_seq), "grp": grp},
            device_id_type=MESH,
        )

    def hop_start(j, value):
        src, dst, _ = hop_refs(j)
        value = value.astype(src.dtype)
        src[...] = value
        dst[...] = value

        def one(k, carry):
            hop_copy(j, k).start()
            return carry

        lax.fori_loop(1, n_seq, one, 0)

    def hop_end(j):
        def one(k, carry):
            hop_copy(j, k).wait()
            return carry

        lax.fori_loop(1, n_seq, one, 0)
        _, _, whole = hop_refs(j)

        def add(i, total):
            return total + whole[i].astype(F32)

        return lax.fori_loop(0, n_seq, add, jnp.zeros((HOP_ROWS[j], 128), F32))

    position = lax.broadcasted_iota(jnp.int32, (channels, rows), 0)
    column = lax.broadcasted_iota(jnp.int32, (channels, rows), 1)
    chosen = jnp.where(position == column + seq * rows, 1.0, 0.0).astype(BF)

    def pick(v):
        return mm_low(v, chosen)

    def film_block(layer, place):
        if place < 4:
            return ff[4 * layer + place]
        return ff[KEY_VALUE + (FILM - 4) * layer + place - 4]

    def film_rows(layer, v, places):
        return jnp.concatenate([mm_low(v, film_block(layer, i)) for i in places], axis=1)

    def film_back(layer, v, places):
        total = None
        for i, place in enumerate(places):
            term = mm_nt_low(v[:, i * WIDE : (i + 1) * WIDE], film_block(layer, place))
            total = term if total is None else total + term
        return mm_nt_low(total, chosen)

    wide_head = channels // HEADS
    copies_of = n_seq // HEADS
    head = lax.div(seq, copies_of)
    lane = lax.broadcasted_iota(jnp.int32, (channels, 128), 1)
    at_row = lax.broadcasted_iota(jnp.int32, (channels, 128), 0)
    of_head = at_row == head * wide_head + lax.rem(lane, wide_head)
    head_columns = jnp.where(of_head, 1.0, 0.0).astype(BF)
    own_half = lax.div(lax.broadcasted_iota(jnp.int32, (8, 128), 1), wide_head) == (
        lax.broadcasted_iota(jnp.int32, (8, 128), 0)
    )

    def exchange(index, source, target):
        def copy(k):
            dest = lax.rem(seq + k, n_seq)
            return pltpu.make_async_remote_copy(
                src_ref=source(dest),
                dst_ref=target,
                send_sem=each_send.at[index, k],
                recv_sem=each_recv.at[index, k],
                device_id={"seq": dest, "grp": grp},
                device_id_type=MESH,
            )

        def begin():
            def one(k, carry):
                copy(k).start()
                return carry

            lax.fori_loop(1, n_seq, one, 0)

        def finish():
            def one(k, carry):
                copy(k).wait()
                return carry

            lax.fori_loop(1, n_seq, one, 0)

        return begin, finish

    kv_begin, kv_finish = exchange(
        0, lambda dest: kv_out.at[lax.div(dest, copies_of)], kv_in.at[seq]
    )
    at_begin, at_finish = exchange(1, lambda dest: at_out.at[dest], at_in.at[seq])
    dq_begin, dq_finish = exchange(3, lambda dest: dq_out, dq_all.at[seq])
    small_begin, small_finish = exchange(2, lambda dest: small_out, small_in.at[seq])

    def head_weights():
        value = kv_in[...].reshape(channels, WIDE)
        return value[:, 0:128], value[:, 128:256]

    def attention():
        keys, values = head_weights()
        pieces = []
        for layer in range(LAYERS):
            high = queries_ref[layer].astype(BF)
            rest = (queries_ref[layer] - high.astype(F32)).astype(BF)
            both = mm(high, head_columns) + mm(rest, head_columns)
            half = lax.div(lax.broadcasted_iota(jnp.int32, both.shape, 1), wide_head)
            pieces.append(jnp.where(half == layer, both, 0.0))
        probe = mm_nt_fine(jnp.concatenate(pieces, axis=0), keys)
        pr = prompt[...]
        scores = mm_nt_fine(probe, pr) * 0.125
        live = lax.broadcasted_iota(jnp.int32, scores.shape, 1) < lengths_ref[pairing_ref[0]]
        scores = jnp.where(live, scores, NEGATIVE)
        weight = jnp.exp(scores - jnp.max(scores, axis=1, keepdims=True))
        value = weight / jnp.sum(weight, axis=1, keepdims=True)
        probs[...] = value
        mean = jnp.concatenate(
            [
                jnp.mean(value[l * number : (l + 1) * number], axis=0, keepdims=True)
                for l in range(LAYERS)
            ]
            + [jnp.zeros((8 - LAYERS, value.shape[1]), F32)],
            axis=0,
        )
        seen = mm_low(mean, pr)
        mixed = jnp.where(own_half, mm_low(seen, values), 0.0)
        left[0:8] = seen
        left[8:16] = mm_nt_low(mixed, head_columns)

    def wblock(layer, place):
        return w[MAIN * layer + place].reshape(channels, WIDE)

    def inside(low, count):
        row = lax.broadcasted_iota(jnp.int32, (count, 1), 0) + (low - HALO) + seq * own
        return (row >= 0) & (row < n_seq * own)

    def windows_forward(layer):
        low = 16 * layer
        high = grid_rows - low
        scale, shift = 1.0 + vec[layer, 0:1], vec[layer, 1:2]
        here = xe[...].astype(F32) if layer == 0 else x1[...]
        shifted = (here * scale + shift).astype(BF).astype(F32)
        shifted = jnp.where(inside(0, grid_rows), shifted, 0.0)
        groups = grid_rows // 8
        bh[0] = jnp.zeros((8, channels), F32)
        bh[1 : 1 + groups] = in_eights(shifted)
        bh[1 + groups :] = jnp.zeros((3, 8, channels), F32)
        sht[layer] = jnp.transpose(shifted[HALO:top]).astype(BF)
        cat[low:high, channels : 2 * channels] = shifted[low:high].astype(BF)
        for tap in (0, 2):
            start = 8 + low + (tap - 1) * dil_ref[layer]
            cat[low:high, tap * channels : (tap + 1) * channels] = window(
                bh, start, high - low, channels
            ).astype(BF)

    def gates(layer, first_row, rows_now):
        spot = slice(first_row, first_row + rows_now)
        value = cat[spot, 0:2048]
        for part in range(2):
            columns = slice(part * WIDE, (part + 1) * WIDE)
            base = MAIN * layer + 5 * part
            lhs = mm(value, w[base : base + 4].reshape(2048, WIDE))
            tangent = jnp.tanh(lhs + vec[layer, 2:3, columns])
            rhs = mm(value, w[base + 10 : base + 14].reshape(2048, WIDE))
            opening = jax.nn.sigmoid(rhs + vec[layer, 3:4, columns])
            gate = tangent * opening
            gated[spot, columns] = gate.astype(BF)
            slopes[layer, spot, columns] = (opening * (1.0 - tangent * tangent)).astype(BF)
            other = slice(channels + part * WIDE, channels + (part + 1) * WIDE)
            slopes[layer, spot, other] = (gate * (1.0 - opening)).astype(BF)

    def residual(layer, first_row, rows_now):
        value = gated[first_row : first_row + rows_now]
        for part in range(2):
            columns = slice(part * WIDE, (part + 1) * WIDE)
            term = mm(value, wblock(layer, 5 * part + 4))
            if layer == 0:
                base = xe[first_row : first_row + rows_now, columns].astype(F32)
                x1[first_row : first_row + rows_now, columns] = (base + term) * HALF_ROOT
            else:
                base = x1[first_row : first_row + rows_now, columns]
                x1[first_row : first_row + rows_now, columns] = (base + term) * HALF_ROOT

    def skipped(layer, first_row, rows_now):
        value = gated[first_row : first_row + rows_now]
        spot = slice(first_row - HALO, first_row - HALO + rows_now)
        for part in range(2):
            columns = slice(part * WIDE, (part + 1) * WIDE)
            term = mm(value, wblock(layer, 5 * part + 14))
            if layer == 0:
                sk[spot, columns] = term
            else:
                sk[spot, columns] = sk[spot, columns] + term

    low, high = 16, grid_rows - 16

    def gate_grads(layer, first_row, rows_now):
        spot = slice(first_row, first_row + rows_now)
        bb[spot, 0:channels] = (bx[spot] * HALF_ROOT).astype(BF)
        branch = jnp.concatenate([wblock(layer, 5 * part + 4) for part in range(4)], axis=1)
        back = mm_nt(bb[spot], branch)
        keep = inside(first_row, rows_now)
        for side in range(2):
            columns = slice(side * channels, (side + 1) * channels)
            value = back * slopes[layer, spot, columns].astype(F32)
            middle = slice((2 + side) * channels, (3 + side) * channels)
            cat[spot, middle] = jnp.where(keep, value, 0.0).astype(BF)

    def windows_backward(layer):
        reach, limit = (low, high) if layer else (HALO, top)
        edge = 1 + low // 8
        bh[0:edge] = jnp.zeros((edge, 8, channels), F32)
        bh[1 + high // 8 :] = jnp.zeros((edge + 2, 8, channels), F32)
        for side in range(2):
            middle = slice((2 + side) * channels, (3 + side) * channels)
            value = cat[low:high, middle].astype(F32)
            bh[edge : 1 + high // 8] = in_eights(value)
            total = jnp.sum(value[HALO - low : top - low], axis=0, keepdims=True)
            sums[layer, 2 + side : 3 + side] = total
            for tap in (0, 2):
                start = 8 + reach - (tap - 1) * dil_ref[layer]
                columns = slice((2 * tap + side) * channels, (2 * tap + side + 1) * channels)
                cat[reach:limit, columns] = window(bh, start, limit - reach, channels).astype(BF)

    def frame_grads(layer, first_row, rows_now):
        spot = slice(first_row, first_row + rows_now)
        taps = jnp.concatenate(
            [wblock(layer, 5 * part + tap) for tap in range(3) for part in range(4)], axis=1
        )
        back = mm_nt(cat[spot], taps)
        if layer:
            here = x1[spot]
            row = lax.broadcasted_iota(jnp.int32, (rows_now, 1), 0) + first_row
            kept = jnp.where((row >= HALO) & (row < top), back, 0.0)
        else:
            here = xe[spot].astype(F32)
            kept = back
        sums[layer, 0:1] += jnp.sum(kept * here, axis=0, keepdims=True)
        sums[layer, 1:2] += jnp.sum(kept, axis=0, keepdims=True)
        bx[spot] = bx[spot] * HALF_ROOT + back * (1.0 + vec[layer, 0:1])

    def weight_grad(layer, part, i):
        if i < 4:
            tap = i if i < 3 else 1
            start = pl.multiple_of(tap * 1024 + part * WIDE, WIDE)
            lhs = sht[layer] if i < 3 else condt[...]
            return mm(lhs, cat[HALO:top, pl.ds(start, WIDE)])
        start = pl.multiple_of(part * WIDE, WIDE)
        return mm(gatt[layer], bb[HALO:top, pl.ds(start, WIDE)])

    core_sent = {}

    def give(layer, xx):
        part = 2 * (1 - c) + xx
        buffer, base = (gs, 0) if layer else (w, MAIN)
        for i in range(5):
            value = weight_grad(layer, part, i).astype(BF)
            buffer[base + 5 * xx + i] = value.reshape(nz, 2, rows, WIDE)
        core_sent[layer, xx] = remote(
            buffer.at[pl.ds(base + 5 * xx, 5)], red_in.at[layer, pl.ds(5 * xx, 5)], seq, sib
        )

    def keep(layer, xx):
        part = 2 * c + xx
        core_sent[layer, xx].wait_recv()
        for i in range(5):
            value = weight_grad(layer, part, i).reshape(nz, 2, rows, WIDE)
            spot = 5 * xx + i
            red_in[layer, spot] = (red_in[layer, spot].astype(F32) + value).astype(BF)

    ones, twos, zs, targets = {}, {}, {}, {}
    for layer in range(LAYERS):
        for k in range(nz):
            zd = lax.rem(z + k, nz)
            targets[layer, k] = (zd, y_first(zd, OUT_SPLIT[layer]))

    def red_one(layer, k):
        zd, a = targets[layer, k]
        b = 1 - a
        ones[layer, k] = []
        for j in range(2):
            xi, yi = a * (1 - x) + b * j, a * j + b * (1 - y)
            ones[layer, k].append(
                remote(
                    red_in.at[layer, pl.ds(5 * xi, 5), zd, yi],
                    one_in.at[layer, k, j],
                    a * seq + b * other_y, a * across + b * grp,
                )
            )

    def red_two(layer, k):
        zd, a = targets[layer, k]
        b = 1 - a
        you = a * y + b * x
        for j in range(2):
            ones[layer, k][j].wait_recv()
            xi, yi = a * x + b * j, a * j + b * y

            def body(i, carry, j=j, xi=xi, yi=yi):
                one_in[layer, k, j, i] = (
                    one_in[layer, k, j, i] + red_in[layer, 5 * xi + i, zd, yi]
                )
                return carry

            lax.fori_loop(0, 5, body, 0)
        twos[layer, k] = remote(
            one_in.at[layer, k, 1 - you], two_in.at[layer, k],
            a * other_y + b * seq, a * grp + b * across,
        )

    def red_three(layer, k):
        zd, a = targets[layer, k]
        you = a * y + (1 - a) * x
        twos[layer, k].wait_recv()

        def body(i, carry):
            two_in[layer, k, i] = two_in[layer, k, i] + one_in[layer, k, you, i]
            return carry

        lax.fori_loop(0, 5, body, 0)
        if k:
            zs[layer, k] = remote(two_in.at[layer, k], z_in.at[layer, k - 1], zd * 2 + y, grp)

    lasts = {}
    outs = []

    def local_out(src, dst):
        copy = pltpu.make_async_copy(src, dst, out_sem.at[len(outs)])
        copy.start()
        outs.append(copy)

    def red_four(layer):
        for k in range(1, nz):
            zs[layer, k].wait_recv()

        def body(i, carry):
            total = two_in[layer, 0, i].astype(F32)
            for k in range(1, nz):
                total = total + z_in[layer, k - 1, i].astype(F32)
            fin[layer, i] = total.astype(BF)
            return carry

        lax.fori_loop(0, 5, body, 0)
        src, dst = fin.at[layer], out_hbm.at[layer, mine]
        lasts[layer] = [remote(src, dst, seq, across), remote(src, dst, seq, sib)]
        if not layer and LAST_DIRECT:
            lasts[layer].append(remote(src, dst, seq, (1 - x) * 2 + 1 - c))
        local_out(src, dst)

    def red_five(layer):
        lasts[layer][0].wait_recv()
        ref = out_hbm.at[layer, theirs]
        lasts[layer].append(remote(ref, ref, seq, sib))

    ops = {}

    def op(*key):
        def keep_op(body):
            ops[key] = body
            return body

        return keep_op

    main_tiles = (0, 1, 2, 3, 4, 5, 6, 7, 15, 16)
    merges, crosses, film_sent, seen, hops = {}, {}, {}, {}, {}
    size_all, size_mid, size_own = grid_rows // 2, (high - low) // 2, own // 2
    embed = same_rows(embed_ref[...].astype(F32))

    for phase in (1, 2):

        @op("prep", phase)
        def _(phase=phase):
            ready([PER_LAYER * (phase - 1) + t for t in main_tiles], prep, BLOCK_OF)
            merges[phase] = merge_start(phase)

        @op("cross", phase)
        def _(phase=phase):
            crosses[phase] = merge_cross(phase, merges[phase])

        @op("end", phase)
        def _(phase=phase):
            merge_end(phase, crosses[phase])
            spread_z(phase)

    def quarter(j):
        return range(j * nz // 4, (j + 1) * nz // 4)

    for phase in (1, 2):
        for j in range(4):
            for name, body in (("first", first), ("second", second), ("third", third)):

                @op(name, phase, j)
                def _(phase=phase, j=j, body=body):
                    for k in quarter(j):
                        body(phase, k)

    parts = {"K": (0, KEY_VALUE), "R": (KEY_VALUE, FILM * LAYERS - KEY_VALUE)}
    for name, (begin, blocks) in parts.items():
        half = blocks // 2
        own_half_at = begin + c * half

        @op("fc" + name)
        def _(name=name, begin=begin, half=half):
            order = FILM_ORDER[:2] if name == "K" else FILM_ORDER[2:]
            for layer in range(LAYERS):
                ready([PER_LAYER * layer + t for t in order], fr, FILM_OF)
            film_sent[name, 0] = remote(
                fr.at[pl.ds(begin + (1 - c) * half, half)],
                fr_in.at[pl.ds(begin // 2, half)],
                seq, sib,
            )

        @op("fx" + name)
        def _(name=name, begin=begin, half=half, own_half_at=own_half_at):
            film_sent[name, 0].wait_recv()
            spot = slice(begin // 2, begin // 2 + half)
            fr_in[spot] = fr_in[spot] + fr[pl.ds(own_half_at, half)]
            ref = pl.ds(begin // 2, half)
            film_sent[name, 1] = remote(fr_in.at[ref], fx.at[ref], seq, across)

        @op("fl" + name)
        def _(name=name, begin=begin, half=half, own_half_at=own_half_at):
            film_sent[name, 1].wait_recv()
            spot = slice(begin // 2, begin // 2 + half)
            ref = pl.ds(own_half_at, half)
            ff[ref] = fr_in[spot] + fx[spot]
            film_sent[name, 2] = remote(ff.at[ref], ff.at[ref], seq, sib)

    for turn in range(4):

        @op("pr", turn)
        def _(turn=turn):
            total = prompt[...] if turn else None
            for i in range(4):
                prompt_copy(turn, i).wait()
                flag = (pairing_ref[0] == 4 * turn + i).astype(F32).astype(BF)
                part = slice((i % 2) * channels, (i % 2 + 1) * channels)
                term = slopes[i // 2, 0 : prompt.shape[0], part] * flag
                total = term if total is None else total + term
            prompt[...] = total
            if turn < 3:
                for i in range(4):
                    prompt_copy(turn + 1, i).start()

    def gathered():
        while gathering:
            gathering.pop().wait_send()

    @op("condt")
    def _():
        local_in[2].wait()
        condt[...] = jnp.transpose(cat[HALO:top, 1536:2048].astype(F32)).astype(BF)

    @op("hsK")
    def _():
        film_sent["K", 2].wait_recv()
        for h in range(HEADS):
            columns = slice((h % 4) * wide_head, (h % 4 + 1) * wide_head)
            pieces = [
                film_block(layer, place + h // 4).astype(F32)[:, columns]
                for place in (0, 2)
                for layer in range(LAYERS)
            ]
            kv_out[h] = jnp.concatenate(pieces, axis=1).astype(BF)
        kv_in[seq] = kv_out[head]
        kv_begin()

    @op("heK")
    def _():
        kv_finish()

    @op("att")
    def _():
        attention()

    @op("hsB")
    def _():
        film_sent["R", 2].wait_recv()
        vectors = []
        embed_here, mixed = pick(embed), pick(left[8:16])
        for layer in range(LAYERS):
            vectors.append(film_rows(layer, mixed, (4, 5))[layer : layer + 1])
            steps = film_rows(layer, embed_here, (10, 11, 12, 13))
            vectors += [steps[0:1, :channels], steps[0:1, channels:]]
        hop_start(0, pack(vectors))

    @op("heB")
    def _():
        total = hop_end(0)
        hops["pooled"] = [unpack(total, 3 * layer) for layer in range(LAYERS)]
        for layer in range(LAYERS):
            vec[layer, 2:3] = unpack(total, 3 * layer + 1)
            vec[layer, 3:4] = unpack(total, 3 * layer + 2)

    @op("hsC")
    def _():
        vectors = []
        for layer in range(LAYERS):
            pooled = hops["pooled"][layer]
            film = film_rows(layer, pick(same_rows(pooled)), (6, 7, 8, 9))
            vectors += [film[0:1, :channels], film[0:1, channels:]]
        hop_start(1, pack(vectors))

    @op("heC")
    def _():
        total = hop_end(1)
        for layer in range(LAYERS):
            vec[layer, 0:1] = unpack(total, 2 * layer)
            vec[layer, 1:2] = unpack(total, 2 * layer + 1)

    @op("win0")
    def _():
        local_in[1].wait()
        for copy in halos[:4]:
            copy.wait_recv()
        windows_forward(0)

    @op("win1")
    def _():
        local_in[3].wait()
        local_in[4].wait()
        for copy in halos[4:]:
            copy.wait_recv()
        bx[...] = bb[:, 0:channels].astype(F32)
        windows_forward(1)

    for layer in range(LAYERS):
        start, size = (low, size_mid) if layer else (0, size_all)
        for part, name in enumerate("ab"):
            first_row = start + part * size

            @op(f"gates{layer}{name}")
            def _(layer=layer, first_row=first_row, size=size, part=part):
                if not part:
                    arrived(1 + layer)
                gates(layer, first_row, size)

        @op(f"gatt{layer}")
        def _(layer=layer):
            gatt[layer] = jnp.transpose(gated[HALO:top].astype(F32)).astype(BF)

    @op("res0")
    def _():
        for part in range(2):
            residual(0, part * size_all, size_all)

    @op("skip0")
    def _():
        for part in range(2):
            skipped(0, HALO + part * size_own, size_own)

    @op("out1")
    def _():
        for part in range(2):
            residual(1, HALO + part * size_own, size_own)
            skipped(1, HALO + part * size_own, size_own)
        local_out(x1.at[pl.ds(HALO, own)], block_hbm.at[0])
        local_out(sk, skip_hbm.at[0])

    for layer in range(LAYERS):
        for part, name in enumerate("ab"):

            @op(f"gg{layer}{name}")
            def _(layer=layer, part=part):
                if layer and not part:
                    sums[...] = jnp.zeros_like(sums)
                gate_grads(layer, low + part * size_mid, size_mid)

            @op(f"fg{layer}{name}")
            def _(layer=layer, part=part):
                if layer:
                    frame_grads(1, low + part * size_mid, size_mid)
                else:
                    frame_grads(0, HALO + part * size_own, size_own)

        @op(f"winb{layer}")
        def _(layer=layer):
            windows_backward(layer)

        for xx in range(2):

            @op("give", layer, xx)
            def _(layer=layer, xx=xx):
                if not layer:
                    gathered()
                give(layer, xx)

            @op("keep", layer, xx)
            def _(layer=layer, xx=xx):
                keep(layer, xx)

        for j in range(4):
            for name, body in (("one", red_one), ("two", red_two), ("three", red_three)):

                @op(name, layer, j)
                def _(layer=layer, j=j, body=body):
                    for k in quarter(j):
                        body(layer, k)

        @op("four", layer)
        def _(layer=layer):
            red_four(layer)

        @op("five", layer)
        def _(layer=layer):
            red_five(layer)

    @op("hs3")
    def _():
        local_out(bx.at[pl.ds(HALO, own)], gframes_hbm.at[0])
        hop_start(2, pack([sums[l, i : i + 1] for l in range(LAYERS) for i in range(4)]))

    @op("he3")
    def _():
        total = hop_end(2)
        hops["sides"] = [[unpack(total, 4 * l + i) for i in range(4)] for l in range(LAYERS)]

    @op("hs4")
    def _():
        vectors = []
        for layer in range(LAYERS):
            dfilm = same_rows(jnp.concatenate(hops["sides"][layer][0:2], axis=1))
            vectors.append(film_back(layer, dfilm, (6, 7, 8, 9))[0:1])
        hop_start(3, pack(vectors))

    @op("he4")
    def _():
        total = hop_end(3)
        hops["dpooled"] = [unpack(total, layer) for layer in range(LAYERS)]


    @op("fb")
    def _():
        vectors = [
            film_back(l, same_rows(hops["dpooled"][l]), (4, 5))[0:1] for l in range(LAYERS)
        ]
        if copies_of > 1:
            hop_start(4, pack(vectors))
            total = hop_end(4)
            vectors = [unpack(total, layer) for layer in range(LAYERS)]
        dmixed = jnp.concatenate(vectors + [jnp.zeros((8 - LAYERS, channels), F32)], axis=0)
        dmixed = jnp.where(own_half, mm_low(dmixed, head_columns), 0.0)
        keys, values = head_weights()
        pr = prompt[...]
        dmean = mm_nt_low(mm_nt_low(dmixed, values), pr) * (1.0 / number)
        dprobs = jnp.concatenate(
            [jnp.broadcast_to(dmean[l : l + 1], (number, channels)) for l in range(LAYERS)], axis=0
        )
        value = probs[...]
        inner = jnp.sum(dprobs * value, axis=1, keepdims=True)
        dprobe = mm_low(value * (dprobs - inner) * 0.125, pr)
        dqueries = mm_low(dprobe, keys)
        half = lax.div(lax.broadcasted_iota(jnp.int32, (number, 128), 1), wide_head)
        dquery = jnp.where(half == 0, dqueries[0:number], dqueries[number : 2 * number])
        dq_in[grp] = dquery.astype(BF)
        small_out[...] = jnp.concatenate([dmixed, jnp.zeros((8, 128), F32)], axis=0).astype(BF)
        lefts = jnp.concatenate(
            [dprobe, left[0:2], left[8:10]]
            + [hops["pooled"][layer] for layer in range(LAYERS)]
            + [embed[0:1], jnp.zeros((128 - 2 * number - 7, channels), F32)],
            axis=0,
        )
        at_out[...] = jnp.transpose(lefts).astype(BF).reshape(n_seq, rows, 128)

    @op("hs5")
    def _():
        small_in[seq] = small_out[...]
        at_in[seq] = at_out[seq]
        small_begin()
        at_begin()

    def halves(one, two):
        wanted = lax.broadcasted_iota(jnp.int32, one.shape, 1) < wide_head
        return (
            jnp.where(wanted, one, pltpu.roll(two, wide_head, 1)),
            jnp.where(wanted, pltpu.roll(one, wide_head, 1), two),
        )

    def by_heads(ref):
        blocks = [[], []]
        for h in range(0, HEADS, 2):
            pair = halves(ref[h * copies_of].astype(F32), ref[(h + 1) * copies_of].astype(F32))
            for layer in range(LAYERS):
                blocks[layer].append(pair[layer])
        return [jnp.concatenate(blocks[layer], axis=1) for layer in range(LAYERS)]

    dq_sent = []

    @op("dq1")
    def _():
        for k in range(1, 4):
            ref = dq_in.at[grp]
            dq_sent.append(remote(ref, ref, seq, lax.rem(grp + k, 4)))

    @op("dq2")
    def _():
        for copy in dq_sent:
            copy.wait_recv()
        total = dq_in[0].astype(F32)
        for k in range(1, 4):
            total = total + dq_in[k].astype(F32)
        dq_out[...] = total
        dq_all[seq] = total
        dq_begin()

    @op("dq3")
    def _():
        dq_finish()
        total = by_heads(dq_all)
        for layer in range(LAYERS):
            dquery_ref[layer] = total[layer]

    @op("he5")
    def _():
        small_finish()
        at_finish()

        full = by_heads(small_in)
        pieces = []
        for layer in range(LAYERS):
            pieces += hops["sides"][layer]
            pieces += [hops["dpooled"][layer], full[layer][layer : layer + 1]]
        pieces.append(jnp.zeros((16 - len(pieces), channels), F32))
        wide[grp] = jnp.concatenate(pieces, axis=0).astype(BF)
        at = lax.broadcasted_iota(jnp.int32, (rows, 128), 1)
        thin = jnp.where(at >= 66, at_in[seq].astype(F32), 0.0)
        for h in range(0, HEADS, 2):
            one, two = at_in[h * copies_of].astype(F32), at_in[(h + 1) * copies_of].astype(F32)
            pair = jnp.where(at < wide_head, one, pltpu.roll(two, wide_head, 1))
            bundle[grp, :, h * wide_head : (h + 2) * wide_head] = pair.astype(BF)
            for k, value in ((h, one), (h + 1, two)):
                turned = pltpu.roll(value, wide_head + 2 * k, 1)
                thin = jnp.where(lax.div(at, 2) == k, turned, thin)
        bundle[grp, :, channels : channels + 128] = thin.astype(BF)

    bundles = []

    @op("bundle")
    def _():
        for k in range(1, 4):
            for ref in (bundle.at[grp], wide.at[grp]):
                bundles.append(remote(ref, ref, seq, lax.rem(grp + k, 4)))

    @op("low")
    def _():
        for copy in bundles:
            copy.wait_recv()
        mask = head_mask()
        at = lax.broadcasted_iota(jnp.int32, (8, channels), 0)
        probe = bundle[0, :, 0:channels].astype(F32)
        for k in range(1, 4):
            probe = probe + bundle[k, :, 0:channels].astype(F32)
        probe = probe.astype(BF)
        blank = jnp.zeros((number, channels), F32)
        column = lax.div(lax.broadcasted_iota(jnp.int32, (number, channels), 1), wide_head)
        for layer in range(LAYERS):
            side = []
            for h in range(HEADS):
                one = jnp.where(column == h, queries_ref[layer], 0.0)
                side += [blank, one] if layer else [one, blank]
            low_ref[layer, 0] = mm(probe, jnp.concatenate(side, axis=0).astype(BF)).astype(BF)
            total = None
            for k in range(4):
                right = wide[k].astype(F32)[6 * layer : 6 * layer + 6]
                dmixed = jnp.where(mask, right[5:6], 0.0)
                nothing = jnp.zeros((1, channels), F32)
                rows_of = []
                for h in range(HEADS):
                    one = dmixed[h : h + 1]
                    rows_of += [nothing, one] if layer else [one, nothing]
                value = jnp.concatenate(rows_of, axis=0)
                gap = jnp.zeros((48, channels), F32)
                rest = jnp.zeros((56, channels), F32)
                pieces = [jnp.concatenate([value, gap, jnp.zeros((64, channels), F32)], axis=0)]
                for i, row in ((4, 2), (0, 4), (1, 4), (2, 6), (3, 6)):
                    row = row + (layer if row < 6 else 0)
                    one = jnp.where(at == row, right[i : i + 1], 0.0)
                    pieces.append(
                        jnp.concatenate([jnp.zeros((64, channels), F32), one, rest], axis=0)
                    )
                term = mm(
                    bundle[k, :, channels : channels + 128],
                    jnp.concatenate(pieces, axis=1).astype(BF),
                )
                total = term if total is None else total + term
            for i in range(6):
                low_ref[layer, 1 + i] = total[:, i * channels : (i + 1) * channels].astype(BF)

    @op("end")
    def _():
        for copies in lasts.values():
            for copy in copies[1:]:
                copy.wait_recv()
        if LAST_DIRECT:
            lasts[0][0].wait_recv()
        for copy in outs:
            copy.wait()
        for copy in halos:
            copy.wait_send()
        gathered()
        for copy in waits:
            copy.wait_send()

    local_in[0].wait()
    for key in ORDER:
        ops[key if isinstance(key, tuple) else (key,)]()


def train_step(
    n_seq, owners, dilations, lengths, pairing, step_embed, queries, master, prompts,
    frames_in, cond_frames, grad_out, grad_skip,
):
    _, own, channels = frames_in.shape
    rows = master.shape[1]
    number = queries.shape[1]
    grid_rows = own + 2 * HALO
    nz = n_seq // 2
    v = pltpu.VMEM
    dma = pltpu.SemaphoreType.DMA
    frame_out = jax.ShapeDtypeStruct((1, own, channels), F32)
    film = FILM * LAYERS
    copies = 52 + 24 * nz
    return pl.pallas_call(
        functools.partial(step_kernel, n_seq),
        out_shape=(
            frame_out,
            frame_out,
            frame_out,
            jax.ShapeDtypeStruct((LAYERS, 4, 5, rows, WIDE), BF),
            jax.ShapeDtypeStruct((LAYERS, LOW_RANK, rows, channels), BF),
            jax.ShapeDtypeStruct((LAYERS, number, channels), F32),
        ),
        in_specs=[smem_spec()] * 4 + [vmem_spec()] * 2 + [any_spec()] * 6,
        out_specs=(any_spec(),) * 4 + (vmem_spec(),) * 2,
        scratch_shapes=[
            v((BLOCKS, nz, 2, rows, WIDE), BF),
            v((10, nz, 2, rows, WIDE), BF),
            v((BLOCKS, rows, WIDE), BF),
            v((BLOCKS // 2, rows, WIDE), BF),
            v((BLOCKS // 4, rows, WIDE), BF),
            v((film, rows, WIDE), BF),
            v((film // 2, rows, WIDE), BF),
            v((film // 2, rows, WIDE), BF),
            v((film, rows, WIDE), BF),
            v((LAYERS, 10, nz, 2, rows, WIDE), BF),
            v((LAYERS, nz, 2, 5, rows, WIDE), BF),
            v((LAYERS, nz, 5, rows, WIDE), BF),
            v((LAYERS, nz - 1, 5, rows, WIDE), BF),
            v((LAYERS, 5, rows, WIDE), BF),
            v((grid_rows, channels), BF),
            v((grid_rows, 6 * channels), BF),
            v((LAYERS, grid_rows, 2 * channels), BF),
            v((grid_rows, channels), BF),
            v((grid_rows, channels), F32),
            v((grid_rows // 8 + 4, 8, channels), F32),
            v((grid_rows, 2 * channels), BF),
            v((LAYERS, channels, own), BF),
            v((channels, own), BF),
            v((LAYERS, channels, own), BF),
            v((grid_rows, channels), F32),
            v((own, channels), F32),
            v(master.shape, F32),
            v(prompts.shape[1:], BF),
            v((LAYERS * number, prompts.shape[1]), F32),
            v((16, channels), F32),
            v((LAYERS, 8, channels), F32),
            v((LAYERS, 8, channels), F32),
            v((4, rows, channels + 128), BF),
            v((4, 16, channels), BF),
            v((4, number, 128), BF),
            v((HEADS, rows, WIDE), BF),
            v((n_seq, rows, WIDE), BF),
            v((n_seq, rows, 128), BF),
            v((n_seq, rows, 128), BF),
            v((16, 128), BF),
            v((n_seq, 16, 128), BF),
            v((number, 128), F32),
            v((n_seq, number, 128), F32),
            v((sum(HOP_ROWS), 128), F32),
            v((n_seq, sum(HOP_ROWS), 128), F32),
            dma((5,)),
            dma((4,)),
            dma((8,)),
            dma((8,)),
            dma((8,)),
            dma((copies,)),
            dma((copies,)),
            dma((len(HOP_ROWS), n_seq)),
            dma((len(HOP_ROWS), n_seq)),
            dma((4, n_seq)),
            dma((4, n_seq)),
        ],
        compiler_params=pltpu.CompilerParams(
            collective_id=0, has_side_effects=True, vmem_limit_bytes=MEM
        ),
        name="train_step",
    )(
        owners, dilations, lengths, pairing, step_embed, queries, master, prompts,
        frames_in, cond_frames, grad_out, grad_skip,
    )


def adam_update(weight, moment_one, moment_two, gradient, step_rate):
    moment_one = BETA_ONE * moment_one + (1.0 - BETA_ONE) * gradient
    moment_two = BETA_TWO * moment_two + (1.0 - BETA_TWO) * gradient * gradient
    normal = (
        moment_one
        * (1.0 / (1.0 - BETA_ONE**STEP))
        / (jnp.sqrt(moment_two * (1.0 / (1.0 - BETA_TWO**STEP))) + EPSILON)
    )
    return (moment_one, moment_two, weight - step_rate * (normal + WEIGHT_DECAY * weight))


def update_kernel(
    owners_ref, master_hbm, first_hbm, second_hbm, grad_hbm, low_hbm,
    queries_ref, qfirst_ref, qsecond_ref, dq_ref, block_in, skip_in, gframes_in,
    nfirst_hbm, nsecond_hbm, nmaster_hbm, ncopy_hbm, nqfirst_ref, nqsecond_ref, nqueries_ref,
    block_out, skip_out, gframes_out,
    master, first, second, grad, low, three, one, two, copied, frames,
    tile_of, grad_sem, in_sem, out_sem, frame_sem,
):
    grp = lax.axis_index("grp")
    grads_in = [
        pltpu.make_async_copy(a, b, grad_sem.at[i])
        for i, (a, b) in enumerate(((grad_hbm, grad), (low_hbm, low)))
    ]
    spots = [pl.ds(start, count) for start, count in CHUNKS]
    slots_in = [
        [
            pltpu.make_async_copy(a.at[spot], b.at[spot], in_sem.at[i, j])
            for j, (a, b) in enumerate(
                ((master_hbm, master), (first_hbm, first), (second_hbm, second))
            )
        ]
        for i, spot in enumerate(spots)
    ]
    frames_in = [
        pltpu.make_async_copy(a, frames.at[i], frame_sem.at[0, i])
        for i, a in enumerate((block_in, skip_in, gframes_in))
    ]
    for copy in grads_in + slots_in[0]:
        copy.start()
    for copies in slots_in[1:]:
        for copy in copies:
            copy.start()
    for copy in frames_in:
        copy.start()

    for slot in range(CAP + 1):
        tile_of[slot] = TILES
    count = jnp.int32(0)
    for tile in range(TILES):
        own = owners_ref[tile] == grp

        @pl.when(own)
        def _(count=count, tile=tile):
            tile_of[jnp.minimum(count, CAP)] = tile

        count = count + own.astype(jnp.int32)
    news = adam_update(
        queries_ref[...], qfirst_ref[...], qsecond_ref[...], dq_ref[...], QUERY_RATE
    )
    nqfirst_ref[...], nqsecond_ref[...], nqueries_ref[...] = news

    def slot_update(slot, carry):
        tile = tile_of[slot]
        used = (tile < TILES).astype(jnp.int32)
        tile = jnp.minimum(tile, TILES - 1)
        layer, kind = lax.div(tile, PER_LAYER), lax.rem(tile, PER_LAYER)
        plain = kind < 8
        pair = jnp.where(plain, lax.rem(kind, 2), (kind == 16).astype(jnp.int32))
        tap = jnp.where(plain, lax.div(kind, 2), 4)
        full = jnp.concatenate([grad[layer, 2 * pair, tap], grad[layer, 2 * pair + 1, tap]], axis=1)
        place = jnp.where(kind < 10, kind - 3, kind - 10)
        thin = low[layer, jnp.clip(place, 0, LOW_RANK - 1)]
        is_thin = ((kind >= 8) & (kind <= 14)).astype(jnp.int32)
        gradient = jnp.where(
            jnp.broadcast_to(is_thin, full.shape) > 0, thin.astype(F32), full.astype(F32)
        )
        old, old_first, old_second = master[slot], first[slot], second[slot]
        new_first, new_second, new = adam_update(old, old_first, old_second, gradient, LEARN_RATE)
        keep = jnp.broadcast_to(used, old.shape) > 0
        new = jnp.where(keep, new, old)
        one[slot] = jnp.where(keep, new_first, old_first)
        two[slot] = jnp.where(keep, new_second, old_second)
        three[slot] = new
        copied[slot] = new.astype(BF)
        return carry

    for copy in grads_in:
        copy.wait()
    outs = []
    for i, (start, number) in enumerate(CHUNKS):
        for copy in slots_in[i]:
            copy.wait()
        lax.fori_loop(start, start + number, slot_update, 0)
        for j, (a, b) in enumerate(
            ((one, nfirst_hbm), (two, nsecond_hbm), (three, nmaster_hbm), (copied, ncopy_hbm))
        ):
            copy = pltpu.make_async_copy(a.at[spots[i]], b.at[spots[i]], out_sem.at[i, j])
            copy.start()
            outs.append(copy)
    for i, target in enumerate((block_out, skip_out, gframes_out)):
        frames_in[i].wait()
        copy = pltpu.make_async_copy(frames.at[i], target, frame_sem.at[1, i])
        copy.start()
        outs.append(copy)
    for copy in outs:
        copy.wait()


CHUNKS = ((0, 2), (2, 3), (5, 4), (9, 4))


def update(owners, master, first, second, grads, low, queries, qfirst, qsecond, dq, *frames):
    any_, whole = any_spec(), vmem_spec()
    query = jax.ShapeDtypeStruct(queries.shape, F32)
    full = jax.ShapeDtypeStruct(master.shape, F32)
    passed = jax.ShapeDtypeStruct(frames[0].shape, F32)
    v = pltpu.VMEM
    slots = v(master.shape, F32)
    return pl.pallas_call(
        update_kernel,
        out_shape=(full, full, full, jax.ShapeDtypeStruct(master.shape, BF), query, query, query)
        + (passed,) * 3,
        in_specs=[smem_spec()] + [any_] * 5 + [whole] * 4 + [any_] * 3,
        out_specs=(any_,) * 4 + (whole,) * 3 + (any_,) * 3,
        scratch_shapes=[
            slots, slots, slots, v(grads.shape, BF), v(low.shape, BF),
            slots, slots, slots, v(master.shape, BF), v((3,) + passed.shape, F32),
            pltpu.SMEM((CAP + 1,), jnp.int32),
            pltpu.SemaphoreType.DMA((2,)),
            pltpu.SemaphoreType.DMA((len(CHUNKS), 3)),
            pltpu.SemaphoreType.DMA((len(CHUNKS), 4)),
            pltpu.SemaphoreType.DMA((2, 3)),
        ],
        compiler_params=pltpu.CompilerParams(vmem_limit_bytes=MEM),
        name="update",
    )(owners, master, first, second, grads, low, queries, qfirst, qsecond, dq, *frames)


def on_device(
    n_seq,
    frames_in,
    cond_frames,
    step_embed,
    prompts,
    prompt_lengths,
    pairing,
    dilations,
    owners,
    master,
    first_moment,
    second_moment,
    queries,
    query_first,
    query_second,
    grad_out,
    grad_skip,
):
    block, skip, gframes, own_grads, low, dq = train_step(
        n_seq, owners, dilations, prompt_lengths, pairing, step_embed, queries, master, prompts,
        frames_in, cond_frames, grad_out, grad_skip,
    )
    (
        new_first, new_second, new_master, new_copy, nqf, nqs, nq,
        block_out, skip_out, grad_frames,
    ) = update(
        owners, master, first_moment, second_moment, own_grads, low,
        queries, query_first, query_second, dq, block, skip, gframes,
    )
    return (
        new_first, new_second, new_master, new_copy, nqf, nqs, nq,
        block_out, skip_out, grad_frames,
    )


def solution(mesh):
    shard = P("grp", "seq", None)
    placed = (
        shard, shard, P("grp", None), P(), P(), P("grp"), P(), P(),
        shard, shard, shard, P(), P(), P(), shard, shard,
    )
    return jax.shard_map(
        functools.partial(on_device, mesh.shape["seq"]),
        mesh=mesh,
        in_specs=placed,
        out_specs=(shard, shard, shard, shard, P(), P(), P(), shard, shard, shard),
        check_vma=False,
    )
```

profile of v0, /device:TPU:9, one launch (start us, length us, event | category | flops | bytes accessed | tf_op | source)
XLA Modules:
  0.0 168.8 jit_solution(14112208075061991962)
XLA Ops:
  1.3 156.8 %train_step.1 = (f32[1,640,512]{2,1,0:T(8,128)}, f32[1,640,512]{2,1,0:T(8,128)}, f32[1,640,512]{2,1,0:T(8,128)}, bf16[2,4,5,64,256]{4,3,2,1,0:T(8,128)(2,1)}, bf...) custom-call(s32[34]{0:T(128)} %owners_ref.3, s32[2]{0:T(128)} %dil_ref.1, s32[16]{0:T(128)} %lengths_ref.1, ...), custom_call_target="tpu_custom_call" | custom-call | tf_op jit(solution)/shard_map/train_step/pallas_call | solution.py:1229
  158.1 10.5 %update.1 = (f32[13,64,512]{2,1,0:T(8,128)}, f32[13,64,512]{2,1,0:T(8,128)}, f32[13,64,512]{2,1,0:T(8,128)}, bf16[13,64,512]{2,1,0:T(8,128)(2,1)}, f32[2,32,512]...) custom-call(s32[34]{0:T(128)} %owners_ref.3, ...), custom_call_target="tpu_custom_call" | custom-call | tf_op jit(solution)/shard_map/update/pallas_call | solution.py:1428
where the time goes:
time: 169 us
  Pallas kernels  167 us (99%)
    pallas_call x1, Pallas kernels, train_step(): pl.pallas_call(functools.partial(step_kernel, n_seq), out_shape=(frame_ou...  157 us
    pallas_call x1, Pallas kernels, update(): pl.pallas_call(update_kernel, out_shape=(full, full, full, jax.ShapeDtype...  10.5 us

commit v1 on v0

--- a/solution.py
+++ b/solution.py
@@ -1319,11 +1319,11 @@
 
 def update_kernel(
     owners_ref, master_hbm, first_hbm, second_hbm, grad_hbm, low_hbm,
-    queries_ref, qfirst_ref, qsecond_ref, dq_ref, block_in, skip_in, gframes_in,
-    nfirst_hbm, nsecond_hbm, nmaster_hbm, ncopy_hbm, nqfirst_ref, nqsecond_ref, nqueries_ref,
+    queries_hbm, qfirst_hbm, qsecond_hbm, dq_hbm, block_in, skip_in, gframes_in,
+    nfirst_hbm, nsecond_hbm, nmaster_hbm, ncopy_hbm, nqfirst_hbm, nqsecond_hbm, nqueries_hbm,
     block_out, skip_out, gframes_out,
-    master, first, second, grad, low, three, one, two, copied, frames,
-    tile_of, grad_sem, in_sem, out_sem, frame_sem,
+    master, first, second, grad, low, three, one, two, copied, frames, asked,
+    tile_of, grad_sem, in_sem, out_sem, frame_sem, asked_sem,
 ):
     grp = lax.axis_index("grp")
     grads_in = [
@@ -1344,13 +1344,15 @@
         pltpu.make_async_copy(a, frames.at[i], frame_sem.at[0, i])
         for i, a in enumerate((block_in, skip_in, gframes_in))
     ]
-    for copy in grads_in + slots_in[0]:
+    asked_in = [
+        pltpu.make_async_copy(a, asked.at[i], asked_sem.at[i])
+        for i, a in enumerate((queries_hbm, qfirst_hbm, qsecond_hbm, dq_hbm))
+    ]
+    for copy in grads_in + slots_in[0] + asked_in + frames_in[:1] + slots_in[1] + frames_in[1:]:
         copy.start()
-    for copies in slots_in[1:]:
+    for copies in slots_in[2:]:
         for copy in copies:
             copy.start()
-    for copy in frames_in:
-        copy.start()
 
     for slot in range(CAP + 1):
         tile_of[slot] = TILES
@@ -1363,10 +1365,16 @@
             tile_of[jnp.minimum(count, CAP)] = tile
 
         count = count + own.astype(jnp.int32)
-    news = adam_update(
-        queries_ref[...], qfirst_ref[...], qsecond_ref[...], dq_ref[...], QUERY_RATE
-    )
-    nqfirst_ref[...], nqsecond_ref[...], nqueries_ref[...] = news
+    outs = []
+
+    def send(a, b, sem):
+        copy = pltpu.make_async_copy(a, b, sem)
+        copy.start()
+        outs.append(copy)
+
+    def pass_frames(i, target):
+        frames_in[i].wait()
+        send(frames.at[i], target, frame_sem.at[1, i])
 
     def slot_update(slot, carry):
         tile = tile_of[slot]
@@ -1395,7 +1403,7 @@
 
     for copy in grads_in:
         copy.wait()
-    outs = []
+    passed = (block_out, skip_out, gframes_out)
     for i, (start, number) in enumerate(CHUNKS):
         for copy in slots_in[i]:
             copy.wait()
@@ -1403,14 +1411,18 @@
         for j, (a, b) in enumerate(
             ((one, nfirst_hbm), (two, nsecond_hbm), (three, nmaster_hbm), (copied, ncopy_hbm))
         ):
-            copy = pltpu.make_async_copy(a.at[spots[i]], b.at[spots[i]], out_sem.at[i, j])
-            copy.start()
-            outs.append(copy)
-    for i, target in enumerate((block_out, skip_out, gframes_out)):
-        frames_in[i].wait()
-        copy = pltpu.make_async_copy(frames.at[i], target, frame_sem.at[1, i])
-        copy.start()
-        outs.append(copy)
+            send(a.at[spots[i]], b.at[spots[i]], out_sem.at[i, j])
+        if i < len(passed):
+            pass_frames(i, passed[i])
+        if i == 1:
+            for copy in asked_in:
+                copy.wait()
+            news = adam_update(asked[0], asked[1], asked[2], asked[3], QUERY_RATE)
+            for j, (value, target) in enumerate(
+                zip(news, (nqfirst_hbm, nqsecond_hbm, nqueries_hbm))
+            ):
+                asked[4 + j] = value
+                send(asked.at[4 + j], target, asked_sem.at[4 + j])
     for copy in outs:
         copy.wait()
 
@@ -1419,7 +1431,7 @@
 
 
 def update(owners, master, first, second, grads, low, queries, qfirst, qsecond, dq, *frames):
-    any_, whole = any_spec(), vmem_spec()
+    any_ = any_spec()
     query = jax.ShapeDtypeStruct(queries.shape, F32)
     full = jax.ShapeDtypeStruct(master.shape, F32)
     passed = jax.ShapeDtypeStruct(frames[0].shape, F32)
@@ -1429,16 +1441,18 @@
         update_kernel,
         out_shape=(full, full, full, jax.ShapeDtypeStruct(master.shape, BF), query, query, query)
         + (passed,) * 3,
-        in_specs=[smem_spec()] + [any_] * 5 + [whole] * 4 + [any_] * 3,
-        out_specs=(any_,) * 4 + (whole,) * 3 + (any_,) * 3,
+        in_specs=[smem_spec()] + [any_] * 12,
+        out_specs=(any_,) * 10,
         scratch_shapes=[
             slots, slots, slots, v(grads.shape, BF), v(low.shape, BF),
             slots, slots, slots, v(master.shape, BF), v((3,) + passed.shape, F32),
+            v((7,) + queries.shape, F32),
             pltpu.SMEM((CAP + 1,), jnp.int32),
             pltpu.SemaphoreType.DMA((2,)),
             pltpu.SemaphoreType.DMA((len(CHUNKS), 3)),
             pltpu.SemaphoreType.DMA((len(CHUNKS), 4)),
             pltpu.SemaphoreType.DMA((2, 3)),
+            pltpu.SemaphoreType.DMA((7,)),
         ],
         compiler_params=pltpu.CompilerParams(vmem_limit_bytes=MEM),
         name="update",

time: 169 us -> 167 us (0.988)
  no operation moved by 1% of the time
where the time goes in v1:
time: 167 us
  Pallas kernels  166 us (99%)
    pallas_call x1, Pallas kernels, train_step(): pl.pallas_call(functools.partial(step_kernel, n_seq), out_shape=(frame_ou...  157 us
    pallas_call x1, Pallas kernels, update(): pl.pallas_call(update_kernel, out_shape=(full, full, full, jax.ShapeDtype...  8.96 us

profile of v1, /device:TPU:9, one launch (start us, length us, event | category | flops | bytes accessed | tf_op | source)
XLA Modules:
  0.0 167.3 jit_solution(7903133061200914536)
XLA Ops:
  1.3 156.8 %train_step.1 = (f32[1,640,512]{2,1,0:T(8,128)}, f32[1,640,512]{2,1,0:T(8,128)}, f32[1,640,512]{2,1,0:T(8,128)}, bf16[2,4,5,64,256]{4,3,2,1,0:T(8,128)(2,1)}, bf...) custom-call(s32[34]{0:T(128)} %owners_ref.3, s32[2]{0:T(128)} %dil_ref.1, s32[16]{0:T(128)} %lengths_ref.1, ...), custom_call_target="tpu_custom_call" | custom-call | tf_op jit(solution)/shard_map/train_step/pallas_call | solution.py:1229
  158.1 9.0 %update.1 = (f32[13,64,512]{2,1,0:T(8,128)}, f32[13,64,512]{2,1,0:T(8,128)}, f32[13,64,512]{2,1,0:T(8,128)}, bf16[13,64,512]{2,1,0:T(8,128)(2,1)}, f32[2,32,512]...) custom-call(s32[34]{0:T(128)} %owners_ref.3, ...), custom_call_target="tpu_custom_call" | custom-call | tf_op jit(solution)/shard_map/update/pallas_call | solution.py:1440
